TPU v7x, 32 devices: a whole 2x2x4 slice. The times are simulated.
32 devices in a mesh: pipe: 4 (over y, core), expert: 8 (over z, x).
Axes of the slice: x: 2, y: 2, z: 4, core: 2. Of those that a mesh axis runs over, the one named last changes fastest.
Arguments:
- tokens_a: bfloat16 [4, 1024, 2048], P('pipe', 'expert'), may hold values from -6 to 6
- cotangent_a: bfloat16 [4, 1024, 2048], P('pipe', 'expert'), may hold values from -6 to 6
- tokens_b: bfloat16 [4, 1024, 2048], P('pipe', 'expert'), may hold values from -6 to 6
- routes_a: int32 [4, 1024, 2], P('pipe', 'expert'), may hold values from 0 to 7, as said below
- routes_b: int32 [4, 1024, 2], P('pipe', 'expert'), may hold values from 0 to 7, as said below
- probs_a: float32 [4, 1024, 2], P('pipe', 'expert'), may hold values from 0.1 to 0.9
- probs_b: float32 [4, 1024, 2], P('pipe', 'expert'), may hold values from 0.1 to 0.9
- w_gate: bfloat16 [4, 8, 2048, 768], P('pipe', 'expert'), may hold values from -0.125 to 0.125
- w_up: bfloat16 [4, 8, 2048, 768], P('pipe', 'expert'), may hold values from -0.125 to 0.125
- w_down: bfloat16 [4, 8, 768, 2048], P('pipe', 'expert'), may hold values from -0.21875 to 0.21875
Outputs:
- grad_a: bfloat16 [4, 1024, 2048], P('pipe', 'expert')
- grad_b: bfloat16 [4, 1024, 2048], P('pipe', 'expert')
Inputs may be any that keep to these rules, and one draw needn't show every extreme that they name: `routes_a`: in every section one expert, drawn per section, is named exactly 56 times by the 128 tokens of every aligned block of 128 tokens; no block names any expert more than 56 times; the two experts of a token differ. `routes_b`: in every section one expert, drawn per section, is named exactly 56 times by the 128 tokens of every aligned block of 128 tokens; no block names any expert more than 56 times; the two experts of a token differ.
All inputs are finite; a program needn't handle non-finite values.
Results may differ from a plain program's by a relative error of at most 0.0062.
Values may be sent and summed in bfloat16 or wider, within the bound.
A program may use at most 64 MiB of HBM per device.

v0:
```python
import jax
import jax.numpy as jnp
from jax import lax
from jax.sharding import PartitionSpec as P


def shifted(block, axis, distance):
    devices = range(lax.axis_size(axis))
    route = [((i - distance) % len(devices), i) for i in devices]
    return lax.ppermute(block, axis, route)


def slot_table(routes, experts):
    route_hits = (routes[:, :, None] == jnp.arange(experts, dtype=jnp.int32)[None, None, :]).astype(
        jnp.int32
    )
    per_token = jnp.sum(route_hits, axis=1)
    before = jnp.cumsum(per_token, axis=0) - per_token
    return jnp.sum(route_hits * before[:, None, :], axis=2)


def slot_hits(routes, experts, capacity):
    slot_index = slot_table(routes, experts)
    flat_ids = routes * capacity + slot_index
    targets = jnp.arange(experts * capacity, dtype=jnp.int32)
    return (flat_ids[:, :, None] == targets[None, None, :]).astype(jnp.bfloat16)


def place_tokens(tokens, hits, experts, capacity):
    table = jnp.sum(hits, axis=1)
    packed = lax.dot_general(
        table, tokens, (((0,), (0,)), ((), ())), preferred_element_type=jnp.float32
    )
    return packed.astype(jnp.bfloat16).reshape(experts, capacity, tokens.shape[1])


def place_scaled(cotangent, probs, hits, experts, capacity):
    width = cotangent.shape[1]
    rows = (
        (probs[:, :, None] * cotangent[:, None, :].astype(jnp.float32))
        .astype(jnp.bfloat16)
        .reshape(-1, width)
    )
    flat_hits = hits.reshape(-1, experts * capacity)
    packed = lax.dot_general(
        flat_hits, rows, (((0,), (0,)), ((), ())), preferred_element_type=jnp.float32
    )
    return packed.astype(jnp.bfloat16).reshape(experts, capacity, width)


def recompute(flat_rows, gate_mat, up_mat):
    gate_pre = jnp.dot(flat_rows, gate_mat, preferred_element_type=jnp.float32)
    up_pre = jnp.dot(flat_rows, up_mat, preferred_element_type=jnp.float32)
    return (gate_pre, up_pre)


def backprop(gate_pre, up_pre, flat_scaled, gate_mat, up_mat, down_mat):
    contract = (((1,), (1,)), ((), ()))
    d_hidden = lax.dot_general(flat_scaled, down_mat, contract, preferred_element_type=jnp.float32)
    gate_sig = jax.nn.sigmoid(gate_pre)
    active = gate_pre * gate_sig
    slope = gate_sig * (1.0 + gate_pre * (1.0 - gate_sig))
    d_gate = (d_hidden * up_pre * slope).astype(jnp.bfloat16)
    d_up = (d_hidden * active).astype(jnp.bfloat16)
    back = lax.dot_general(d_gate, gate_mat, contract, preferred_element_type=jnp.float32)
    back = back + lax.dot_general(d_up, up_mat, contract, preferred_element_type=jnp.float32)
    return back.astype(jnp.bfloat16)


def on_device(
    tokens_a, cotangent_a, tokens_b, routes_a, routes_b, probs_a, probs_b, w_gate, w_up, w_down
):
    experts = lax.axis_size("expert")
    tok_count = tokens_a.shape[1]
    width = tokens_a.shape[2]
    capacity = 7 * tok_count // (2 * experts)
    gate_mat = w_gate[0, 0]
    up_mat = w_up[0, 0]
    down_mat = w_down[0, 0]
    first_hits = slot_hits(routes_a[0], experts, capacity)
    second_hits = slot_hits(routes_b[0], experts, capacity)
    first_cot = cotangent_a[0]
    first_tokens = place_tokens(tokens_a[0], first_hits, experts, capacity)
    first_scaled = place_scaled(first_cot, probs_a[0], first_hits, experts, capacity)

    def give_back(result_rows, hits, cotangent):
        returned = lax.all_to_all(result_rows, "expert", split_axis=0, concat_axis=0, tiled=True)
        table = jnp.sum(hits, axis=1)
        picked = jnp.dot(table, returned.reshape(-1, width), preferred_element_type=jnp.float32)
        summed = cotangent.astype(jnp.float32) + picked
        return summed.astype(jnp.bfloat16)

    def flat_grad(arrived_tokens, arrived_scaled):
        lead_shape = arrived_tokens.shape[:2]
        gate_pre, up_pre = recompute(arrived_tokens.reshape(-1, width), gate_mat, up_mat)
        grad_rows = backprop(
            gate_pre, up_pre, arrived_scaled.reshape(-1, width), gate_mat, up_mat, down_mat
        )
        return grad_rows.reshape(lead_shape + (width,))

    def expert_items(pieces):
        return flat_grad(pieces[0], pieces[1])

    def one_batch(sent_tokens, sent_scaled):
        return expert_items(
            (
                lax.all_to_all(sent_tokens, "expert", split_axis=0, concat_axis=0, tiled=True),
                lax.all_to_all(sent_scaled, "expert", split_axis=0, concat_axis=0, tiled=True),
            )
        )

    grad_a = give_back(one_batch(first_tokens, first_scaled), first_hits, first_cot)
    second_cot = shifted(grad_a, "pipe", -1)
    second_tokens = place_tokens(tokens_b[0], second_hits, experts, capacity)
    second_scaled = place_scaled(second_cot, probs_b[0], second_hits, experts, capacity)
    grad_b = give_back(one_batch(second_tokens, second_scaled), second_hits, second_cot)
    return (grad_a[None], grad_b[None])


def solution(mesh):
    in_specs = (
        P("pipe", "expert", None),
        P("pipe", "expert", None),
        P("pipe", "expert", None),
        P("pipe", "expert", None),
        P("pipe", "expert", None),
        P("pipe", "expert", None),
        P("pipe", "expert", None),
        P("pipe", "expert", None, None),
        P("pipe", "expert", None, None),
        P("pipe", "expert", None, None),
    )
    out_specs = (P("pipe", "expert", None), P("pipe", "expert", None))
    return jax.shard_map(
        on_device, mesh=mesh, in_specs=in_specs, out_specs=out_specs, check_vma=False
    )
```

profile of v0, /device:TPU:0, one launch (start us, length us, event | category | flops | bytes accessed | tf_op | source)
XLA Modules:
  0.0 328.0 jit_solution(4608510671018547349)
XLA Ops:
  0.7 0.8 convert_reduce_fusion.1
  1.8 0.7 select_reduce_fusion.1
  2.6 0.7 multiply_add_fusion.1
  3.2 1.1 bitcast_convert_fusion.2
  4.4 2.0 bitcast_convert_fusion.1
  6.4 7.3 %all-to-all-start = ((bf16[8,56,2048]{2,1,0:T(8,128)(2,1)}), bf16[8,56,2048]{2,1,0:T(8,128)(2,1)}, u32[]{:S(2)}, u32[]{:S(2)}) async-start(bf16[8,56,2048]{2,1,0:T(8,128)(2,1)} %bitcast.94), calls=%async_computation | async-start | bytes 3670016 | tf_op jit(solution)/shard_map/all_to_all | solution.py:108
  13.7 2.9 convolution_convert_fusion.1
  16.6 39.8 %all-to-all-done = bf16[8,56,2048]{2,1,0:T(8,128)(2,1)} async-done(((bf16[8,56,2048]{2,1,0:T(8,128)(2,1)}), bf16[8,56,2048]{2,1,0:T(8,128)(2,1)}, u32[]{:S(2)}, u32[]{:S(2)}) %all-to-all-start) | async-done | bytes 1835040 | tf_op jit(solution)/shard_map/all_to_all | solution.py:108
  56.4 4.3 %all-to-all-start.1 = ((bf16[8,56,2048]{2,1,0:T(8,128)(2,1)}), bf16[8,56,2048]{2,1,0:T(8,128)(2,1)}, u32[]{:S(2)}, u32[]{:S(2)}) async-start(bf16[8,56,2048]{2,1,0:T(8,128)(2,1)} %bitcast.93), calls=%async_computation.1 | async-start | bytes 3670016 | tf_op jit(solution)/shard_map/all_to_all | solution.py:107
  60.7 5.2 %fusion.18 = f32[448,768]{1,0:T(8,128)} fusion(bf16[448,2048]{1,0:T(8,128)(2,1)} %bitcast.6, bf16[1,1,768,2048]{3,2,1,0:T(8,128)(2,1)} %param.19), kind=kOutput, calls=%fused_computation.22 | convolution fusion | flops 1409286144 | bytes 6356992 | tf_op jit(solution)/shard_map/dot_general | solution.py:59
  65.9 37.0 %all-to-all-done.1 = bf16[8,56,2048]{2,1,0:T(8,128)(2,1)} async-done(((bf16[8,56,2048]{2,1,0:T(8,128)(2,1)}), bf16[8,56,2048]{2,1,0:T(8,128)(2,1)}, u32[]{:S(2)}, u32[]{:S(2)}) %all-to-all-start.1) | async-done | bytes 1835040 | tf_op jit(solution)/shard_map/all_to_all | solution.py:107
  102.9 5.1 %fusion.6 = f32[448,768]{1,0:T(8,128)} fusion(bf16[448,2048]{1,0:T(8,128)(2,1)} %bitcast.10, bf16[1,1,2048,768]{3,2,1,0:T(8,128)(2,1)} %param.17), kind=kOutput, calls=%fused_computation.10 | convolution fusion | flops 1409286144 | bytes 6356992 | tf_op jit(solution)/shard_map/dot_general | solution.py:52
  108.0 8.6 %fusion.4 = f32[448,2048]{1,0:T(8,128)} fusion(bf16[1,1,2048,768]{3,2,1,0:T(8,128)(2,1)} %param.17, f32[448,768]{1,0:T(8,128)} %fusion.6, f32[448,768]{1,0:T(8,128)} %fusion.18, bf16[448,2048]{1,0:T(8,128)(2,1)} %bitcast.10, bf16[1,1,2048,768]{3,2,1,0:T(8,128)(2,1)S(1)} %copy-done), kind=kOutput, calls=%fused_computation.8 | convolution fusion | flops 2822012928 | bytes 14548992 | tf_op jit(solution)/shard_map/dot_general | solution.py:65
  116.6 5.8 %add_convert_fusion.1 = bf16[448,2048]{1,0:T(8,128)(2,1)} fusion(f32[448,2048]{1,0:T(8,128)} %fusion.4, bf16[1,1,2048,768]{3,2,1,0:T(8,128)(2,1)S(1)} %copy-done, f32[448,768]{1,0:T(8,128)} %fusion.18, f32[448,768]{1,0:T(8,128)} %fusion.6), kind=kOutput, calls=%fused_computation.3 | convolution fusion | flops 1413185536 | bytes 11403264 | tf_op jit(solution)/shard_map/dot_general | solution.py:66
  122.4 4.5 %all-to-all-start.2 = ((bf16[8,56,2048]{2,1,0:T(8,128)(2,1)}), bf16[8,56,2048]{2,1,0:T(8,128)(2,1)}, u32[]{:S(2)}, u32[]{:S(2)}) async-start(bf16[8,56,2048]{2,1,0:T(8,128)(2,1)} %bitcast.96), calls=%async_computation.2 | async-start | bytes 3670016 | tf_op jit(solution)/shard_map/all_to_all | solution.py:87
  127.3 2.9 convolution_convert_fusion
  130.3 38.8 %all-to-all-done.2 = bf16[8,56,2048]{2,1,0:T(8,128)(2,1)} async-done(((bf16[8,56,2048]{2,1,0:T(8,128)(2,1)}), bf16[8,56,2048]{2,1,0:T(8,128)(2,1)}, u32[]{:S(2)}, u32[]{:S(2)}) %all-to-all-start.2) | async-done | bytes 1835040 | tf_op jit(solution)/shard_map/all_to_all | solution.py:87
  169.1 4.3 %all-to-all-start.4 = ((bf16[8,56,2048]{2,1,0:T(8,128)(2,1)}), bf16[8,56,2048]{2,1,0:T(8,128)(2,1)}, u32[]{:S(2)}, u32[]{:S(2)}) async-start(bf16[8,56,2048]{2,1,0:T(8,128)(2,1)} %bitcast.91), calls=%async_computation.4 | async-start | bytes 3670016 | tf_op jit(solution)/shard_map/all_to_all | solution.py:107
  173.4 2.1 fusion.24
  175.5 0.2 collective-permute-start
  175.7 6.7 %collective-permute-done = bf16[128,2048]{1,0:T(8,128)(2,1)S(1)} collective-permute-done((bf16[128,2048]{1,0:T(8,128)(2,1)S(1)}, bf16[128,2048]{1,0:T(8,128)(2,1)S(1)}, u32[]{:S(2)}, u32[]{:S(2)}) %collective-permute-start) | collective-permute-done | bytes 524320 | tf_op jit(solution)/shard_map/ppermute | solution.py:10
  182.4 0.8 copy-done.1
  183.3 2.0 bitcast_convert_fusion
  185.3 30.3 %all-to-all-done.4 = bf16[8,56,2048]{2,1,0:T(8,128)(2,1)} async-done(((bf16[8,56,2048]{2,1,0:T(8,128)(2,1)}), bf16[8,56,2048]{2,1,0:T(8,128)(2,1)}, u32[]{:S(2)}, u32[]{:S(2)}) %all-to-all-start.4) | async-done | bytes 1835040 | tf_op jit(solution)/shard_map/all_to_all | solution.py:107
  215.6 4.5 %all-to-all-start.3 = ((bf16[8,56,2048]{2,1,0:T(8,128)(2,1)}), bf16[8,56,2048]{2,1,0:T(8,128)(2,1)}, u32[]{:S(2)}, u32[]{:S(2)}) async-start(bf16[8,56,2048]{2,1,0:T(8,128)(2,1)} %bitcast.92), calls=%async_computation.3 | async-start | bytes 3670016 | tf_op jit(solution)/shard_map/all_to_all | solution.py:108
  220.1 5.2 %fusion.2 = f32[448,768]{1,0:T(8,128)} fusion(bf16[448,2048]{1,0:T(8,128)(2,1)} %bitcast.23, bf16[1,1,2048,768]{3,2,1,0:T(8,128)(2,1)} %param.17), kind=kOutput, calls=%fused_computation.6 | convolution fusion | flops 1409286144 | bytes 6356992 | tf_op jit(solution)/shard_map/dot_general | solution.py:52
  225.3 37.0 %all-to-all-done.3 = bf16[8,56,2048]{2,1,0:T(8,128)(2,1)} async-done(((bf16[8,56,2048]{2,1,0:T(8,128)(2,1)}), bf16[8,56,2048]{2,1,0:T(8,128)(2,1)}, u32[]{:S(2)}, u32[]{:S(2)}) %all-to-all-start.3) | async-done | bytes 1835040 | tf_op jit(solution)/shard_map/all_to_all | solution.py:108
  262.3 5.1 %fusion.16 = f32[448,768]{1,0:T(8,128)} fusion(bf16[448,2048]{1,0:T(8,128)(2,1)} %bitcast.20, bf16[1,1,768,2048]{3,2,1,0:T(8,128)(2,1)} %param.19), kind=kOutput, calls=%fused_computation.20 | convolution fusion | flops 1409286144 | bytes 6356992 | tf_op jit(solution)/shard_map/dot_general | solution.py:59
  267.4 8.6 %fusion = f32[448,2048]{1,0:T(8,128)} fusion(bf16[1,1,2048,768]{3,2,1,0:T(8,128)(2,1)} %param.17, f32[448,768]{1,0:T(8,128)} %fusion.2, f32[448,768]{1,0:T(8,128)} %fusion.16, bf16[448,2048]{1,0:T(8,128)(2,1)} %bitcast.23, bf16[1,1,2048,768]{3,2,1,0:T(8,128)(2,1)S(1)} %copy-done), kind=kOutput, calls=%fused_computation.4 | convolution fusion | flops 2822012928 | bytes 14548992 | tf_op jit(solution)/shard_map/dot_general | solution.py:65
  276.0 4.5 %add_convert_fusion = bf16[448,2048]{1,0:T(8,128)(2,1)S(1)} fusion(f32[448,2048]{1,0:T(8,128)} %fusion, bf16[1,1,2048,768]{3,2,1,0:T(8,128)(2,1)S(1)} %copy-done, f32[448,768]{1,0:T(8,128)} %fusion.16, f32[448,768]{1,0:T(8,128)} %fusion.2), kind=kOutput, calls=%fused_computation.2 | convolution fusion | flops 1413185536 | bytes 11403264 | tf_op jit(solution)/shard_map/dot_general | solution.py:66
  280.5 46.2 %all_to_all.30 = bf16[8,56,2048]{2,1,0:T(8,128)(2,1)S(1)} all-to-all(bf16[8,56,2048]{2,1,0:T(8,128)(2,1)S(1)} %bitcast.97), channel_id=1, replica_groups=mesh['pipe'=4,'expert'=8] {'expert'}, dimensions={0} | all-to-all | bytes 3670016 | tf_op jit(solution)/shard_map/all_to_all | solution.py:87
  326.8 1.3 fusion.26
  (27 shorter events, 0.9 us)
Async XLA Ops:
  0.6 107.4 %copy-start = (bf16[1,1,2048,768]{3,2,1,0:T(8,128)(2,1)S(1)}, bf16[1,1,2048,768]{3,2,1,0:T(8,128)(2,1)}, u32[]{:S(2)}) copy-start(bf16[1,1,2048,768]{3,2,1,0:T(8,128)(2,1)} %param.18) | copy-start | bytes 9437188
  0.6 3.7 %copy-start.5 = (f32[1,128,2]{1,2,0:T(2,128)S(1)}, f32[1,128,2]{1,2,0:T(2,128)}, u32[]{:S(2)}) copy-start(f32[1,128,2]{1,2,0:T(2,128)} %param.15) | copy-start | bytes 3076
  6.4 50.0 %all-to-all-start = ((bf16[8,56,2048]{2,1,0:T(8,128)(2,1)}), bf16[8,56,2048]{2,1,0:T(8,128)(2,1)}, u32[]{:S(2)}, u32[]{:S(2)}) async-start(bf16[8,56,2048]{2,1,0:T(8,128)(2,1)} %bitcast.94), calls=%async_computation | async-start | bytes 3670016 | tf_op jit(solution)/shard_map/all_to_all | solution.py:108
  56.4 46.6 %all-to-all-start.1 = ((bf16[8,56,2048]{2,1,0:T(8,128)(2,1)}), bf16[8,56,2048]{2,1,0:T(8,128)(2,1)}, u32[]{:S(2)}, u32[]{:S(2)}) async-start(bf16[8,56,2048]{2,1,0:T(8,128)(2,1)} %bitcast.93), calls=%async_computation.1 | async-start | bytes 3670016 | tf_op jit(solution)/shard_map/all_to_all | solution.py:107
  122.4 4.5 %copy-start.4 = (s32[1,128,2]{1,2,0:T(2,128)S(1)}, s32[1,128,2]{1,2,0:T(2,128)}, u32[]{:S(2)}) copy-start(s32[1,128,2]{1,2,0:T(2,128)} %param.14) | copy-start | bytes 3076
  122.4 46.7 %all-to-all-start.2 = ((bf16[8,56,2048]{2,1,0:T(8,128)(2,1)}), bf16[8,56,2048]{2,1,0:T(8,128)(2,1)}, u32[]{:S(2)}, u32[]{:S(2)}) async-start(bf16[8,56,2048]{2,1,0:T(8,128)(2,1)} %bitcast.96), calls=%async_computation.2 | async-start | bytes 3670016 | tf_op jit(solution)/shard_map/all_to_all | solution.py:87
  169.1 46.5 %all-to-all-start.4 = ((bf16[8,56,2048]{2,1,0:T(8,128)(2,1)}), bf16[8,56,2048]{2,1,0:T(8,128)(2,1)}, u32[]{:S(2)}, u32[]{:S(2)}) async-start(bf16[8,56,2048]{2,1,0:T(8,128)(2,1)} %bitcast.91), calls=%async_computation.4 | async-start | bytes 3670016 | tf_op jit(solution)/shard_map/all_to_all | solution.py:107
  173.4 9.9 %copy-start.6 = (f32[1,128,2]{1,2,0:T(2,128)S(1)}, f32[1,128,2]{1,2,0:T(2,128)}, u32[]{:S(2)}) copy-start(f32[1,128,2]{1,2,0:T(2,128)} %param.16) | copy-start | bytes 3076
  175.5 7.8 %copy-start.3 = (bf16[128,2048]{1,0:T(8,128)(2,1)}, bf16[128,2048]{1,0:T(8,128)(2,1)S(1)}, u32[]{:S(2)}) copy-start(bf16[128,2048]{1,0:T(8,128)(2,1)S(1)} %fusion.24) | copy-start | bytes 1572868
  175.5 6.9 %collective-permute-start = (bf16[128,2048]{1,0:T(8,128)(2,1)S(1)}, bf16[128,2048]{1,0:T(8,128)(2,1)S(1)}, u32[]{:S(2)}, u32[]{:S(2)}) collective-permute-start(bf16[128,2048]{1,0:T(8,128)(2,1)S(1)} %fusion.24), channel_id=1, source_target_pairs={{8,0},{16,8},{24,16},{0,24},{9,1},{17,9},{25,17},{1,25},{10,2},{18... | collective-permute-start | bytes 1572872 | tf_op jit(solution)/shard_map/ppermute | solution.py:10
  182.4 0.8 copy-start.1
  215.6 46.6 %all-to-all-start.3 = ((bf16[8,56,2048]{2,1,0:T(8,128)(2,1)}), bf16[8,56,2048]{2,1,0:T(8,128)(2,1)}, u32[]{:S(2)}, u32[]{:S(2)}) async-start(bf16[8,56,2048]{2,1,0:T(8,128)(2,1)} %bitcast.92), calls=%async_computation.3 | async-start | bytes 3670016 | tf_op jit(solution)/shard_map/all_to_all | solution.py:108
  280.5 46.2 %copy-start.2 = (bf16[128,2048]{1,0:T(8,128)(2,1)S(1)}, bf16[128,2048]{1,0:T(8,128)(2,1)}, u32[]{:S(2)}) copy-start(bf16[128,2048]{1,0:T(8,128)(2,1)} %copy-done.1) | copy-start | bytes 1572868
where the time goes:
time: 329 us; the launch traced here: 328 us
  waiting for transfers between devices  190 us (58%)
  matrix products  61.2 us (19%)
  blocking collectives  46.2 us (14%)
  starting transfers between devices  25 us (8%)
  other arithmetic  3.97 us (1%)
    all_to_all x2, waiting for transfers between devices, one_batch(): lax.all_to_all(sent_scaled, 'expert', split_axis=0, concat_axis=0, tiled=...  76.8 us
    all_to_all x2, waiting for transfers between devices, one_batch(): lax.all_to_all(sent_tokens, 'expert', split_axis=0, concat_axis=0, tiled=...  67.3 us
    all_to_all x1, blocking collectives, give_back(): lax.all_to_all(result_rows, 'expert', split_axis=0, concat_axis=0, tiled=...  46.2 us
    all_to_all x1, waiting for transfers between devices, give_back(): lax.all_to_all(result_rows, 'expert', split_axis=0, concat_axis=0, tiled=...  38.8 us
    dot_general x2, matrix products, backprop(): lax.dot_general(d_gate, gate_mat, contract, preferred_element_type=jnp.fl...  17.2 us
    all_to_all x2, starting transfers between devices, one_batch(): lax.all_to_all(sent_scaled, 'expert', split_axis=0, concat_axis=0, tiled=...  11.7 us
    dot_general x2, matrix products, backprop(): lax.dot_general(flat_scaled, down_mat, contract, preferred_element_type=j...  10.3 us
    dot_general x2, matrix products, backprop(): lax.dot_general(d_up, up_mat, contract, preferred_element_type=jnp.float32)  10.3 us
  transfers between devices with their start and end apart: 6, of which 6 were waited for; matrix products, arithmetic and copies ran while one was open for 6% of the time, Pallas kernels for 0%

commit v1 on v0

v1 whole, which is shorter than its diff:
```python
import functools

import jax
import jax.numpy as jnp
from jax import lax
from jax.experimental import pallas as pl
from jax.experimental.pallas import tpu as pltpu
from jax.sharding import PartitionSpec as P

ROWS = 4
MESH = pl.DeviceIdType.MESH
F32 = jnp.float32
BF16 = jnp.bfloat16
CHUNKS = 4


def slot_table(routes, experts):
    route_hits = (routes[:, :, None] == jnp.arange(experts, dtype=jnp.int32)[None, None, :]).astype(
        jnp.int32
    )
    per_token = jnp.sum(route_hits, axis=1)
    before = jnp.cumsum(per_token, axis=0) - per_token
    return jnp.sum(route_hits * before[:, None, :], axis=2)


def steps_at(values, size, count):
    found = jnp.zeros_like(values)
    for k in range(1, count):
        found = found + (values >= k * size).astype(jnp.int32)
    return found


def mm(a, b, contract):
    return lax.dot_general(a, b, (contract, ((), ())), preferred_element_type=F32)


NN = ((1,), (0,))
NT = ((1,), (1,))
TN = ((0,), (0,))


def kernel(
    cfg, meta, ta, ca, tb, wg_h, wu_h, wd_h, ga, gb,
    src, metas, wg, wu, wd, pp, fw, sel, sp, inb, pk, fk, nfs, lb, gate, up, dh, dg, du, rb, rp, dn, fd,
    ld_sem, s_m, r_m, s_d, r_d, s_p, r_p, s_f, r_f, s_n, r_n,
    s_b, r_b, s_rp, r_rp, s_rf, r_rf, s_dn, r_fd, s_sh, r_sh,
):
    experts, pipes, cap, tok, width, ff, chunks = cfg
    X = experts // ROWS
    W = width // chunks
    PN, FN, RN = X * cap, 2 * X * cap, 4 * cap
    me = lax.axis_index("expert")
    stage = lax.axis_index("pipe")
    z = me // X
    x = me % X
    odd = z % 2
    p = z + 1 - 2 * odd
    low = z < ROWS // 2
    far = jnp.where(low, 2, 0)
    gateway = jnp.where(low, 2, 1)
    inner = jnp.logical_or(z == 1, z == 2)
    outer = jnp.logical_not(inner)
    sources = (z, p, far, far + 1)

    def dev(zz, xx):
        return {"expert": zz * X + xx}

    def rc(a, b, ss, rs, device):
        return pltpu.make_async_remote_copy(
            src_ref=a, dst_ref=b, send_sem=ss, recv_sem=rs, device_id=device, device_id_type=MESH
        )

    loads = [
        pltpu.make_async_copy(a, b, ld_sem.at[i])
        for i, (a, b) in enumerate(
            (
                (ta, src.at[0]),
                (ca, src.at[1]),
                (tb, src.at[2]),
                (wg_h, wg),
                (wu_h, wu),
                (wd_h, wd),
            )
        )
    ]
    for load in loads:
        load.start()

    barrier = pltpu.get_barrier_semaphore()
    for d in range(1, experts):
        pl.semaphore_signal(
            barrier, inc=1, device_id={"expert": (me + d) % experts}, device_id_type=MESH
        )
    for d in (1, pipes - 1):
        pl.semaphore_signal(
            barrier, inc=1, device_id={"pipe": (stage + d) % pipes}, device_id_type=MESH
        )

    rows_p = lax.broadcasted_iota(jnp.int32, (PN, tok), 0)
    own = meta[...]
    metas[me] = own
    for m in range(2):
        goal = (rows_p + p * PN).astype(F32)
        hit = jnp.logical_or(goal == own[4 * m : 4 * m + 1], goal == own[4 * m + 1 : 4 * m + 2])
        pp[m] = jnp.where(hit, 1.0, 0.0).astype(BF16)
    for i in range(4 * chunks):
        inb[i, PN + tok : 2 * tok] = jnp.zeros((tok - PN, W), BF16)

    @pl.when(outer)
    def _():
        for i in range(4 * chunks):
            inb[i, 2 * tok + FN : 4 * tok] = jnp.zeros((2 * tok - FN, W), BF16)

    pl.semaphore_wait(barrier, experts + 1)

    def meta_copy(d):
        return rc(meta, metas.at[me], s_m.at[d - 1], r_m.at[d - 1], {"expert": (me + d) % experts})

    def meta_arrival(d):
        return rc(
            meta, metas.at[(me - d + experts) % experts], s_m.at[d - 1], r_m.at[d - 1],
            {"expert": (me + d) % experts},
        )

    for d in range(1, experts):
        meta_copy(d).start()

    def cols(c):
        return pl.ds(pl.multiple_of(c * W, W), W)

    def dense_copy(n):
        return rc(
            src.at[n // chunks, :, cols(n % chunks)],
            inb.at[n, pl.ds(pl.multiple_of(2 * tok + tok * odd, tok), tok)],
            s_d.at[n], r_d.at[n, odd], dev(gateway, x),
        )

    def dense_arrival(n, f):
        return rc(
            src.at[n // chunks, :, cols(n % chunks)], inb.at[n, pl.ds((2 + f) * tok, tok)],
            s_d.at[n], r_d.at[n, f], dev(gateway, x),
        )

    def pack_copy(n):
        return rc(pk.at[n], inb.at[n, pl.ds(tok, PN)], s_p.at[n], r_p.at[n], dev(p, x))

    def forward_copy(n):
        return rc(fk.at[n], inb.at[n, pl.ds(2 * tok, FN)], s_f.at[n], r_f.at[n], dev(p, x))

    def block(xx):
        return pl.ds(pl.multiple_of(xx * RN, 16), RN)

    def hop_copy(n, d):
        return rc(
            nfs.at[n, d - 1], lb.at[n, block(x)], s_n.at[n, d - 1], r_n.at[n, d - 1],
            dev(z, (x + d) % X),
        )

    def hop_arrival(n, d):
        return rc(
            nfs.at[n, d - 1], lb.at[n, block((x - d + X) % X)], s_n.at[n, d - 1],
            r_n.at[n, d - 1], dev(z, (x + d) % X),
        )

    def f0(n):
        m = n // (2 * chunks)
        dense_copy(n).start()
        chunk = src[n // chunks, :, cols(n % chunks)]
        pk[n] = mm(pp[m], chunk, NN).astype(BF16)
        pack_copy(n).start()
        inb[n, 0:tok] = chunk

    def f1(n):
        m = n // (2 * chunks)

        @pl.when(inner)
        def _():
            dense_arrival(n, 0).wait_recv()
            dense_arrival(n, 1).wait_recv()
            fk[n] = mm(fw[m], inb[n, 2 * tok : 4 * tok], NN).astype(BF16)
            forward_copy(n).start()

    def f2(n):
        m = n // (2 * chunks)
        pack_copy(n).wait_recv()

        @pl.when(outer)
        def _():
            forward_copy(n).wait_recv()

        for d in range(1, X):
            nfs[n, d - 1] = mm(sel[m, block((x + d) % X)], inb[n], NN).astype(BF16)
            hop_copy(n, d).start()
        lb[n, block(x)] = mm(sel[m, block(x)], inb[n], NN).astype(BF16)

    def tiles(count, body):
        def run(i, carry):
            body(pl.ds(pl.multiple_of(i * 256, 256), 256))
            return carry

        lax.fori_loop(0, count // 256, run, 0)

    def f3_tokens(n):
        for d in range(1, X):
            hop_arrival(n, d).wait_recv()
        c = n % chunks

        def body(part):
            gate[:, part] = gate[:, part] + mm(lb[n], wg[cols(c), part], NN)
            up[:, part] = up[:, part] + mm(lb[n], wu[cols(c), part], NN)

        tiles(ff, body)

    def f3_cot(n):
        for d in range(1, X):
            hop_arrival(n, d).wait_recv()
        c = n % chunks
        m = n // (2 * chunks)
        lb[n] = (lb[n].astype(F32) * sp[m]).astype(BF16)

        def body(part):
            dh[:, part] = dh[:, part] + mm(lb[n], wd[part, cols(c)], NT)

        tiles(ff, body)

    def clear():
        gate[...] = jnp.zeros_like(gate)
        up[...] = jnp.zeros_like(up)

    def middle():
        def body(part):
            g_pre, u_pre, d_hid = gate[:, part], up[:, part], dh[:, part]
            sig = 1.0 / (1.0 + jnp.exp(-g_pre))
            dg[:, part] = (d_hid * u_pre * (sig * (1.0 + g_pre * (1.0 - sig)))).astype(BF16)
            du[:, part] = (d_hid * (g_pre * sig)).astype(BF16)

        tiles(ff, body)

    def held(i):
        return (2 * (i // chunks) + 1) * chunks + i % chunks

    def back_copy(i, d):
        xo = (x + d) % X
        return rc(
            lb.at[held(i), block(xo)], rb.at[i, block(x)], s_b.at[i, d - 1], r_b.at[i, d - 1],
            dev(z, xo),
        )

    def back_arrival(i, d):
        return rc(
            lb.at[held(i), block((x + d) % X)], rb.at[i, block((x - d + X) % X)],
            s_b.at[i, d - 1], r_b.at[i, d - 1], dev(z, (x + d) % X),
        )

    def near_copy(i):
        return rc(
            inb.at[held(i), pl.ds(tok, PN)], rp.at[i, pl.ds(0, PN)], s_rp.at[i], r_rp.at[i], dev(p, x)
        )

    def far_copy(i):
        return rc(
            inb.at[held(i), pl.ds(2 * tok, FN)], rp.at[i, pl.ds(PN, FN)], s_rf.at[i], r_rf.at[i],
            dev(p, x),
        )

    def home_copy(i, f):
        return rc(
            dn.at[i, pl.ds(f * tok, tok)], fd.at[i], s_dn.at[i, f], r_fd.at[i], dev(far + f, x)
        )

    def shift_copy(c):
        return rc(
            ga.at[:, cols(c)], src.at[3, :, cols(c)], s_sh.at[c], r_sh.at[c],
            {"pipe": (stage + pipes - 1) % pipes},
        )

    def r0(i):
        c = i % chunks
        for t in range(W // 256 if W % 256 == 0 else 1):
            size = 256 if W % 256 == 0 else W
            rows = pl.ds(pl.multiple_of(c * W + t * size, size), size)
            both = mm(dg[...], wg[rows, :], NT) + mm(du[...], wu[rows, :], NT)
            lb[held(i), :, t * size : (t + 1) * size] = both.astype(BF16)
        for d in range(1, X):
            back_copy(i, d).start()
        rb[i, block(x)] = lb[held(i), block(x)]

    def r1(i):
        b = i // chunks
        for d in range(1, X):
            back_arrival(i, d).wait_recv()
        inb[held(i)] = mm(sel[b], rb[i], TN).astype(BF16)
        near_copy(i).start()

        @pl.when(outer)
        def _():
            far_copy(i).start()

    def r2(i):
        b = i // chunks

        @pl.when(inner)
        def _():
            far_copy(i).wait_recv()
            both = inb[held(i), 2 * tok : 4 * tok].astype(F32) + mm(fw[b], rp[i, PN : PN + FN], TN)
            dn[i] = both.astype(BF16)
            for f in range(2):
                home_copy(i, f).start()

    def r3(i, k, out):
        b = i // chunks
        c = i % chunks
        near_copy(i).wait_recv()
        home_copy(i, 0).wait_recv()
        total = src[k, :, cols(c)].astype(F32) + inb[held(i), 0:tok].astype(F32)
        total = total + mm(pp[b], rp[i, 0:PN], TN) + fd[i].astype(F32)
        out[:, cols(c)] = total.astype(BF16)

    loads[0].wait()
    f0(0)
    f0(1)
    clear()
    dh[...] = jnp.zeros_like(dh)
    for d in range(1, experts):
        meta_arrival(d).wait_recv()

    def tables(m):
        r = lax.broadcasted_iota(jnp.int32, (X * RN, tok), 0)
        lane = lax.broadcasted_iota(jnp.int32, (X * RN, tok), 1)
        xi = steps_at(r, RN, X)
        rr = r - xi * RN
        q = steps_at(rr, cap, 4)
        j = rr - q * cap
        goal = ((z * X + xi) * cap + j).astype(F32)

        def hits(goal_rows, info):
            return jnp.logical_or(
                goal_rows == info[4 * m : 4 * m + 1], goal_rows == info[4 * m + 1 : 4 * m + 2]
            )

        def put(ref, where, mask):
            ref[m, :, where * tok : (where + 1) * tok] = jnp.where(mask, 1.0, 0.0).astype(BF16)

        put(sel, 0, jnp.logical_and(q == 0, hits(goal, own)))
        put(sel, 1, jnp.logical_and(q == 1, lane == xi * cap + j))
        r_f_rows = lax.broadcasted_iota(jnp.int32, (FN, tok), 0)
        xf = steps_at(r_f_rows, 2 * cap, X)
        rf = r_f_rows - xf * 2 * cap
        ff_ = steps_at(rf, cap, 2)
        goal_f = ((p * X + xf) * cap + rf - ff_ * cap).astype(F32)

        @pl.when(inner)
        def _():
            for f in range(2):
                info = metas[(far + f) * X + x]
                put(sel, 2 + f, jnp.logical_and(q == 2 + f, hits(goal, info)))
                put(fw, f, jnp.logical_and(ff_ == f, hits(goal_f, info)))

        @pl.when(outer)
        def _():
            for f in range(2):
                at = xi * 2 * cap + (q - 2) * cap + j - f * tok
                put(sel, 2 + f, jnp.logical_and(q >= 2, lane == at))

        mine = (me * cap + j).astype(F32)
        total = jnp.zeros((X * RN, tok), F32)
        for xs in range(X):
            for k in range(4):
                info = metas[sources[k] * X + xs]
                here = jnp.logical_and(xi == xs, q == k)
                for route in range(2):
                    ids = info[4 * m + route : 4 * m + route + 1]
                    probs = info[4 * m + 2 + route : 4 * m + 3 + route]
                    hit = jnp.logical_and(here, mine == ids)
                    total = total + jnp.where(hit, probs, 0.0)
        sp[m] = jnp.sum(total, axis=1, keepdims=True)

    tables(0)
    f1(0)
    for load in loads[1:]:
        load.wait()

    def span(lo, hi, body):
        def run(n, carry):
            body(n)
            return carry

        lax.fori_loop(lo, hi, run, 0)

    C = chunks

    def first(n):
        f0(n + 2)
        f1(n + 1)
        f2(n)

        @pl.when(n > 0)
        def _():
            f3_tokens(n - 1)

    def second(n):
        f0(n + 2)
        f1(n + 1)
        f2(n)
        f3_cot(n - 1)

    span(0, C + 1, first)
    tables(1)
    span(C + 1, 2 * C + 1, second)
    middle()
    clear()
    dh[...] = jnp.zeros_like(dh)

    def at(t, lo, body, lag):
        @pl.when(jnp.logical_and(t >= lag, t < lag + C))
        def _():
            body(t - lag + lo)

    def shifted_start(n):
        shift_copy(n % C).wait_recv()
        f0(n)

    def grad_a(i):
        r3(i, 1, ga)
        shift_copy(i).start()

    def third(t):
        at(t, 0, r0, 0)
        at(t, 0, r1, 1)
        at(t, 0, r2, 2)
        at(t, 0, grad_a, 3)
        at(t, 3 * C, shifted_start, 4)

        @pl.when(t + 2 * C + 3 < 3 * C)
        def _():
            f0(t + 2 * C + 3)

        @pl.when(t + 2 * C + 2 < 3 * C)
        def _():
            f1(t + 2 * C + 2)

        @pl.when(t + 2 * C + 1 < 3 * C)
        def _():
            f2(t + 2 * C + 1)

        at(t, 3 * C, f1, 5)
        at(t, 3 * C, f2, 6)
        at(t, 2 * C, f3_tokens, 0)
        at(t, 3 * C, f3_cot, 7)

    span(0, C + 7, third)
    middle()

    def fourth(t):
        at(t, C, r0, 0)
        at(t, C, r1, 1)
        at(t, C, r2, 2)
        at(t, C, lambda i: r3(i, 3, gb), 3)

    span(0, C + 3, fourth)

    def sent(n):
        dense_copy(n).wait_send()
        pack_copy(n).wait_send()
        for d in range(1, X):
            hop_copy(n, d).wait_send()

        @pl.when(inner)
        def _():
            forward_copy(n).wait_send()

    span(0, 4 * C, sent)

    def returned(i):
        for d in range(1, X):
            back_copy(i, d).wait_send()
        near_copy(i).wait_send()

        @pl.when(outer)
        def _():
            far_copy(i).wait_send()

        @pl.when(inner)
        def _():
            for f in range(2):
                home_copy(i, f).wait_send()

    span(0, 2 * C, returned)
    span(0, C, lambda c: shift_copy(c).wait_send())
    for d in range(1, experts):
        meta_copy(d).wait_send()


def on_device(
    tokens_a, cotangent_a, tokens_b, routes_a, routes_b, probs_a, probs_b, w_gate, w_up, w_down
):
    experts = lax.axis_size("expert")
    pipes = lax.axis_size("pipe")
    tok, width = tokens_a.shape[1:]
    ff = w_gate.shape[3]
    cap = 7 * tok // (2 * experts)
    C = CHUNKS
    W = width // C
    X = experts // ROWS
    rows, pn, fn = X * 4 * cap, X * cap, 2 * X * cap

    def info(routes, probs):
        ids = routes[0] * cap + slot_table(routes[0], experts)
        return [ids.astype(F32).T, probs[0].T]

    meta = jnp.concatenate(info(routes_a, probs_a) + info(routes_b, probs_b), axis=0)
    vmem, dma = pltpu.VMEM, pltpu.SemaphoreType.DMA
    out = jax.ShapeDtypeStruct((tok, width), BF16)
    any_spec = pl.BlockSpec(memory_space=pl.ANY)
    vmem_spec = pl.BlockSpec(memory_space=pltpu.VMEM)
    hops = X - 1
    grads = pl.pallas_call(
        functools.partial(kernel, (experts, pipes, cap, tok, width, ff, C)),
        out_shape=(out, out),
        in_specs=[vmem_spec] + [any_spec] * 6,
        out_specs=(vmem_spec, vmem_spec),
        scratch_shapes=[
            vmem((4, tok, width), BF16),
            vmem((experts, 8, tok), F32),
            vmem((width, ff), BF16),
            vmem((width, ff), BF16),
            vmem((ff, width), BF16),
            vmem((2, pn, tok), BF16),
            vmem((2, fn, 2 * tok), BF16),
            vmem((2, rows, 4 * tok), BF16),
            vmem((2, rows, 1), F32),
            vmem((4 * C, 4 * tok, W), BF16),
            vmem((4 * C, pn, W), BF16),
            vmem((4 * C, fn, W), BF16),
            vmem((4 * C, hops, 4 * cap, W), BF16),
            vmem((4 * C, rows, W), BF16),
            vmem((rows, ff), F32),
            vmem((rows, ff), F32),
            vmem((rows, ff), F32),
            vmem((rows, ff), BF16),
            vmem((rows, ff), BF16),
            vmem((2 * C, rows, W), BF16),
            vmem((2 * C, pn + fn, W), BF16),
            vmem((2 * C, 2 * tok, W), BF16),
            vmem((2 * C, tok, W), BF16),
            dma((6,)),
            dma((experts - 1,)),
            dma((experts - 1,)),
            dma((4 * C,)),
            dma((4 * C, 2)),
            dma((4 * C,)),
            dma((4 * C,)),
            dma((4 * C,)),
            dma((4 * C,)),
            dma((4 * C, hops)),
            dma((4 * C, hops)),
            dma((2 * C, hops)),
            dma((2 * C, hops)),
            dma((2 * C,)),
            dma((2 * C,)),
            dma((2 * C,)),
            dma((2 * C,)),
            dma((2 * C, 2)),
            dma((2 * C,)),
            dma((C,)),
            dma((C,)),
        ],
        compiler_params=pltpu.CompilerParams(
            collective_id=0, has_side_effects=True, vmem_limit_bytes=62 * 1024 * 1024
        ),
    )(meta, tokens_a[0], cotangent_a[0], tokens_b[0], w_gate[0, 0], w_up[0, 0], w_down[0, 0])
    return (grads[0][None], grads[1][None])


def solution(mesh):
    spec = P("pipe", "expert", None)
    wspec = P("pipe", "expert", None, None)
    return jax.shard_map(
        on_device,
        mesh=mesh,
        in_specs=(spec,) * 7 + (wspec,) * 3,
        out_specs=(spec, spec),
        check_vma=False,
    )
```

time: 329 us -> 231 us (0.70)
  Pallas kernels: 0 us -> 221 us
  waiting for transfers between devices: 190 us -> 0 us
  matrix products: 61.2 us -> 0 us
  blocking collectives: 46.2 us -> 0 us
  starting transfers between devices: 25 us -> 0 us
    pallas_call x0 -> x1, Pallas kernels: none -> 221 us  [on_device(): pl.pallas_call(functools.partial(kernel, (experts, pipes, cap, tok, width...]
    all_to_all x5 -> x0, waiting for transfers between devices: 183 us -> none  [the longest x2 76.8 us: one_batch(): lax.all_to_all(sent_scaled, 'expert', split_axis=0, concat_axis=0, tiled=...]
    dot_general x14 -> x0, matrix products: 61.2 us -> none  [the longest x2 17.2 us: backprop(): lax.dot_general(d_gate, gate_mat, contract, preferred_element_type=jnp.fl...]
    all_to_all x1 -> x0, blocking collectives: 46.2 us -> none  [give_back(): lax.all_to_all(result_rows, 'expert', split_axis=0, concat_axis=0, tiled=...]
    all_to_all x5 -> x0, starting transfers between devices: 24.8 us -> none  [the longest x2 11.7 us: one_batch(): lax.all_to_all(sent_scaled, 'expert', split_axis=0, concat_axis=0, tiled=...]
    ppermute x1 -> x0, waiting for transfers between devices: 6.7 us -> none  [shifted(): return lax.ppermute(block, axis, route)]
  transfers between devices with their start and end apart: 6 -> 0, of which waited for: 6 -> 0; matrix products, arithmetic and copies ran while one was open for 6% -> 0% of each run, Pallas kernels for 0% -> 0%
where the time goes in v1:
time: 231 us
  Pallas kernels  221 us (96%)
  other arithmetic  5.16 us (2%)
  local copies, waits for them, and re-layouts  4.06 us (2%)
    pallas_call x1, Pallas kernels, on_device(): pl.pallas_call(functools.partial(kernel, (experts, pipes, cap, tok, width...  221 us

profile of v1, /device:TPU:0, one launch (start us, length us, event | category | flops | bytes accessed | tf_op | source)
XLA Modules:
  0.0 230.6 jit_solution(4102741887629061766)
XLA Ops:
  0.6 0.7 convert_reduce_fusion.1
  1.3 0.7 convert_reduce_fusion
  2.0 0.1 copy.17
  2.1 0.1 copy.14
  2.2 0.2 reduce_window_sum.17
  2.4 0.7 select_reduce_fusion.1
  3.2 0.2 reduce_window_sum.18
  3.4 0.7 select_reduce_fusion
  4.1 0.7 convert_bitcast_fusion
  4.8 1.3 pad_maximum_fusion.meta
  6.1 220.8 %shard_map.113 = (bf16[128,2048]{1,0:T(8,128)(2,1)}, bf16[128,2048]{1,0:T(8,128)(2,1)}) custom-call(f32[8,128]{1,0:T(8,128)} %pad_maximum_fusion.meta, bf16[128,2048]{1,0:T(8,128)(2,1)} %bitcast.25, bf16[128,2048]{1,0:T(8,128)(2,1)} %bitcast.26, bf16[128,2048]{1,0:T(8,128)(2,1)} %bitcast.27, bf16[2048,768]{1,0:T(8,128)(2,1)} %bitcast.22, ...), custom_call_target="tpu_custom_call" | custom-call | tf_op jit(solution)/shard_map/pallas_call | solution.py:517
  226.9 1.9 copy.22
  228.8 1.9 copy.23
  (4 shorter events, 0.1 us)

commit v2 on v1

--- a/solution.py
+++ b/solution.py
@@ -11,7 +11,7 @@
 MESH = pl.DeviceIdType.MESH
 F32 = jnp.float32
 BF16 = jnp.bfloat16
-CHUNKS = 4
+CHUNKS = 8
 
 
 def slot_table(routes, experts):

time: 231 us -> 217 us (0.939)
  Pallas kernels: 221 us -> 207 us
    pallas_call x1, Pallas kernels: 221 us -> 207 us  [on_device(): pl.pallas_call(functools.partial(kernel, (experts, pipes, cap, tok, width...]
where the time goes in v2:
time: 217 us
  Pallas kernels  207 us (95%)
  other arithmetic  5.16 us (2%)
  local copies, waits for them, and re-layouts  4.06 us (2%)
    pallas_call x1, Pallas kernels, on_device(): pl.pallas_call(functools.partial(kernel, (experts, pipes, cap, tok, width...  207 us

profile of v2, /device:TPU:0, one launch (start us, length us, event | category | flops | bytes accessed | tf_op | source)
XLA Modules:
  0.0 216.7 jit_solution(10212635251668808044)
XLA Ops:
  0.6 0.7 convert_reduce_fusion.1
  1.3 0.7 convert_reduce_fusion
  2.0 0.1 copy.17
  2.1 0.1 copy.14
  2.2 0.2 reduce_window_sum.17
  2.4 0.7 select_reduce_fusion.1
  3.2 0.2 reduce_window_sum.18
  3.4 0.7 select_reduce_fusion
  4.1 0.7 convert_bitcast_fusion
  4.8 1.3 pad_maximum_fusion.meta
  6.1 206.8 %shard_map.113 = (bf16[128,2048]{1,0:T(8,128)(2,1)}, bf16[128,2048]{1,0:T(8,128)(2,1)}) custom-call(f32[8,128]{1,0:T(8,128)} %pad_maximum_fusion.meta, bf16[128,2048]{1,0:T(8,128)(2,1)} %bitcast.25, bf16[128,2048]{1,0:T(8,128)(2,1)} %bitcast.26, bf16[128,2048]{1,0:T(8,128)(2,1)} %bitcast.27, bf16[2048,768]{1,0:T(8,128)(2,1)} %bitcast.22, ...), custom_call_target="tpu_custom_call" | custom-call | tf_op jit(solution)/shard_map/pallas_call | solution.py:517
  212.9 1.9 copy.22
  214.8 1.9 copy.23
  (4 shorter events, 0.1 us)
